TPU v7x, 32 devices: a whole 2x2x4 slice. The times are simulated.
32 devices in a mesh: grp: 8 (over z, y), col: 4 (over x, core).
Axes of the slice: x: 2, y: 2, z: 4, core: 2. Of those that a mesh axis runs over, the one named last changes fastest.
Arguments:
- window_rows: bfloat16 [122880, 1024], P('grp', 'col'), may hold values from -0.0234375 to 0.0234375
- secular: bfloat16 [122880, 4096], P('grp', 'col'), may hold values from -6 to 6
- source: int32 [122880], P('grp'), may hold values from 0 to 122879, as said below
- kept_count: int32 [1], replicated, may hold values from 61440 to 122879
Outputs:
- merged: bfloat16 [2, 1024, 4096], P(None, 'grp', 'col')
Inputs may be any that keep to these rules, and one draw needn't show every extreme that they name: source is a permutation of 0 to 122879; for j in block b of 15360 indices, source[j] lies in block b or in block b + 4 (b < 4) or b - 4 (b >= 4).
All inputs are finite; a program needn't handle non-finite values.
Results may differ from a plain program's by a relative error of at most 0.0011.
Values may be sent and summed in bfloat16 or wider, within the bound.
A program may use at most 256 MiB of HBM per device.

v0:
```python
import jax
import jax.numpy as jnp
from jax import lax
from jax.sharding import PartitionSpec as P


def partner_2(value, axis, bit):
    mask = 2**bit
    pairs = [(source, source ^ mask) for source in range(lax.axis_size(axis))]
    return lax.ppermute(value, axis, pairs)


def per_device(window_rows, secular, source, kept_count):
    blk = secular.shape[0]
    groups = lax.axis_size("grp")
    pairs = groups // 2
    half_bit = groups.bit_length() - 2
    group_index = lax.axis_index("grp")
    own_base = group_index * blk
    partner_base = jnp.bitwise_xor(group_index, pairs) * blk
    half_index = group_index // pairs
    limit = kept_count[0]
    summed = None
    terms = None
    partner = partner_2(secular, "grp", half_bit)
    stacked = jnp.concatenate([secular, partner], axis=0)
    inside = (source >= own_base) & (source < own_base + blk)
    picks = jnp.where(inside, source - own_base, blk + source - partner_base)
    slab_rows = jnp.where((source < limit)[:, None], stacked[picks], jnp.zeros((), stacked.dtype))
    partial_sum = lax.dot_general(
        lax.all_gather(window_rows, "col", axis=1, tiled=True),
        slab_rows,
        (((0,), (0,)), ((), ())),
        preferred_element_type=jnp.float32,
    )
    upper_flag = (half_index == 0).astype(jnp.float32)
    terms = jnp.stack([partial_sum * upper_flag, partial_sum * (1.0 - upper_flag)])
    summed = lax.psum_scatter(terms, "grp", scatter_dimension=1, tiled=True)
    return summed.astype(jnp.bfloat16)


def solution(mesh):
    return jax.shard_map(
        per_device,
        mesh=mesh,
        in_specs=(P("grp", "col"), P("grp", "col"), P("grp"), P()),
        out_specs=P(None, "grp", "col"),
        check_vma=False,
    )
```

profile of v0, /device:TPU:0, one launch (start us, length us, event | category | flops | bytes accessed | tf_op | source)
XLA Modules:
  0.0 1905.5 jit_solution(3032360808778112428)
XLA Ops:
  6.5 0.0 all-gather.2.cloned.1.call-start
  6.5 0.7 all-gather.2.cloned.1.call-update
  7.3 0.0 reduce-scatter.2.cloned.1.call-start
  7.3 4.1 collective-permute-start
  12.1 0.8 broadcast_compare_fusion
  12.9 0.9 fusion.4
  13.8 1346.9 %collective-permute-done = bf16[15360,1024]{1,0:T(8,128)(2,1)} collective-permute-done((bf16[15360,1024]{1,0:T(8,128)(2,1)}, bf16[15360,1024]{1,0:T(8,128)(2,1)}, u32[]{:S(2)}, u32[]{:S(2)}) %collective-permute-start) | collective-permute-done | bytes 31457312 | tf_op jit(solution)/shard_map/ppermute | solution.py:10
  1360.7 56.5 %pad_maximum_fusion = bf16[30720,1024]{1,0:T(8,128)(2,1)} fusion(bf16[15360,1024]{1,0:T(8,128)(2,1)} %collective-permute-done, bf16[15360,1024]{1,0:T(8,128)(2,1)} %param.5), kind=kLoop, calls=%fused_computation.1 | loop fusion | flops 125829120 | bytes 125829120 | tf_op jit(solution)/shard_map/concatenate | solution.py:26
  1417.1 280.8 %gather_fusion = bf16[15360,1024]{1,0:T(8,128)(2,1)} fusion(bf16[30720,1024]{1,0:T(8,128)(2,1)} %pad_maximum_fusion, s32[15360]{0:T(1024)S(1)} %fusion.4), kind=kCustom, calls=%fused_computation | custom fusion | bytes 62976000 | tf_op jit(solution)/shard_map/gather | solution.py:29
  1698.0 0.0 all-gather.2.cloned.1.call-done
  1698.0 43.6 %multiply_bitcast_fusion.1 = (f32[1,1024,1024]{1,2,0:T(8,128)S(1)}, f32[1,1024,1024]{1,2,0:T(8,128)S(1)}) fusion(f32[]{:T(128)S(6)} %convert_element_type.6, f32[]{:T(128)S(6)} %sub.21, bf16[15360,1024]{1,0:T(8,128)(2,1)} %all-gather.2.cloned.1.call-done, bf16[15360,1024]{1,0:T(8,128)(2,1)} %gather_fusion, pred[15360]{0:T(1024)(128)(4,1)S(1)} %broadcast_compare_fusion), kind=kOutput, calls=%fused_computation.8 | convolution fusion | flops 32230080512 | bytes 71318536 | tf_op jit(solution)/shard_map/dot_general | solution.py:30
  1741.5 4.1 pad_maximum_fusion.1
  1745.6 0.0 reduce-scatter.2.cloned.1.call-update
  1745.6 150.7 %reduce-scatter.2.cloned.1.call-done = f32[2,128,1024]{1,2,0:T(8,128)} async-done(((f32[2,1024,1024]{1,2,0:T(8,128)}), f32[2,128,1024]{1,2,0:T(8,128)}) %reduce-scatter.2.cloned.1.call-update) | async-done | bytes 1048592 | tf_op jit(solution)/shard_map/reduce_scatter | solution.py:38
  1896.3 1.3 convert_element_type.7
  1897.6 1.0 copy.5
Async XLA Ops:
  6.5 1691.5 %all-gather.2.cloned.1.call-start = ((), (), s32[]{:S(2)}) async-start(), calls=%async_computation.1 | async-start | bytes 39321600 | tf_op jit(solution)/shard_map/all_gather | solution.py:31
  7.3 1889.1 %reduce-scatter.2.cloned.1.call-start = ((), (), s32[]{:S(2)}) async-start(), calls=%async_computation.2 | async-start | bytes 9437184 | tf_op jit(solution)/shard_map/reduce_scatter | solution.py:38
  7.3 1353.4 %collective-permute-start = (bf16[15360,1024]{1,0:T(8,128)(2,1)}, bf16[15360,1024]{1,0:T(8,128)(2,1)}, u32[]{:S(2)}, u32[]{:S(2)}) collective-permute-start(bf16[15360,1024]{1,0:T(8,128)(2,1)} %param.5), channel_id=1, source_target_pairs={{0,16},{4,20},{8,24},{12,28},{16,0},{20,4},{24,8},{28,12},{1,17},{... | collective-permute-start | bytes 94371848 | tf_op jit(solution)/shard_map/ppermute | solution.py:10
Sparse Core Ops, SparseCore 0:
  8.9 196.5 all-gather.1
  1745.8 150.5 reduce-scatter.1
where the time goes:
time: 1910 us
  waiting for transfers between devices  1500 us (79%)
  local copies, waits for them, and re-layouts  282 us (15%)
  other arithmetic  63.6 us (3%)
  matrix products  43.6 us (2%)
    ppermute x1, waiting for transfers between devices, partner_2(): return lax.ppermute(value, axis, pairs)  1350 us
    gather x1, local copies, waits for them, and re-layouts, per_device(): stacked[picks]  281 us
    reduce_scatter x1, waiting for transfers between devices, per_device(): summed = lax.psum_scatter(terms, 'grp', scatter_dimension=1, tiled=True)  151 us
    concatenate x1, other arithmetic, per_device(): stacked = jnp.concatenate([secular, partner], axis=0)  56.5 us
    dot_general x1, matrix products, per_device(): lax.dot_general(lax.all_gather(window_rows, 'col', axis=1, tiled=True), s...  43.6 us
  transfers between devices with their start and end apart: 3, of which 2 were waited for; matrix products, arithmetic and copies ran while one was open for 18% of the time, Pallas kernels for 0%

commit v1 on v0

v1 whole, which is shorter than its diff:
```python
import functools

import jax
import jax.numpy as jnp
from jax import lax
from jax.experimental import pallas as pl
from jax.experimental.pallas import tpu as pltpu
from jax.sharding import PartitionSpec as P

UNROLL = 16
TILE = 64


def partner_2(value, axis, bit):
    mask = 2**bit
    pairs = [(source, source ^ mask) for source in range(lax.axis_size(axis))]
    return lax.ppermute(value, axis, pairs)


def invert_kernel(blk, base_ref, own_ref, partner_ref, inverse_ref):
    base = base_ref[0]

    def run(source_ref, first):
        def body(step, carry):
            for k in range(UNROLL):
                j = step * UNROLL + k
                place = source_ref[j] - base
                inside = (place >= 0) & (place < blk)
                inverse_ref[jnp.where(inside, place, blk)] = j + first
            return carry

        lax.fori_loop(0, blk // UNROLL, body, 0)

    run(own_ref, 0)
    run(partner_ref, blk)


def invert(base, own_source, partner_source):
    blk = own_source.shape[0]
    smem = pl.BlockSpec(memory_space=pltpu.SMEM)
    inverse = pl.pallas_call(
        functools.partial(invert_kernel, blk),
        out_shape=jax.ShapeDtypeStruct((blk + 128,), jnp.int32),
        in_specs=[smem] * 3,
        out_specs=smem,
        cost_estimate=pl.CostEstimate(flops=8 * blk, bytes_accessed=12 * blk, transcendentals=0),
    )(base.reshape(1), own_source, partner_source)
    return inverse[:blk]


def pick_kernel(blk, inverse_ref, own_ref, partner_ref, out_ref, wide_ref, stage_ref):
    def widen(step, carry):
        rows = pl.ds(pl.multiple_of(step * 256, 256), 256)
        wide_ref[rows, :] = own_ref[rows, :].astype(jnp.float32)
        wide_ref[pl.ds(pl.multiple_of(blk + step * 256, 256), 256), :] = partner_ref[rows, :].astype(jnp.float32)
        return carry

    lax.fori_loop(0, blk // 256, widen, 0)

    def pick(step, carry):
        first = pl.multiple_of(step * TILE, TILE)
        for k in range(TILE):
            stage_ref[pl.ds(k, 1), :] = wide_ref[pl.ds(inverse_ref[first + k], 1), :]
        out_ref[pl.ds(first, TILE), :] = stage_ref[...].astype(out_ref.dtype)
        return carry

    lax.fori_loop(0, blk // TILE, pick, 0)


def pick_rows(inverse, own, partner):
    blk, wide = own.shape
    vmem = pl.BlockSpec(memory_space=pltpu.VMEM)
    return pl.pallas_call(
        functools.partial(pick_kernel, blk),
        out_shape=jax.ShapeDtypeStruct((blk, wide), own.dtype),
        in_specs=[pl.BlockSpec(memory_space=pltpu.SMEM), vmem, vmem],
        out_specs=vmem,
        scratch_shapes=[
            pltpu.VMEM((2 * blk, wide), jnp.float32),
            pltpu.VMEM((TILE, wide), jnp.float32),
        ],
        compiler_params=pltpu.CompilerParams(vmem_limit_bytes=40 * 2**20),
        cost_estimate=pl.CostEstimate(flops=2 * blk * wide, bytes_accessed=64 * blk * wide, transcendentals=0),
    )(inverse, own, partner)


def scatter_sum(terms):
    return lax.psum_scatter(jnp.stack(terms), "grp", scatter_dimension=1, tiled=True)


def per_device(window_rows, secular, source, kept_count):
    blk, wide = window_rows.shape
    groups = lax.axis_size("grp")
    halves = 2
    half_bit = groups.bit_length() - 2
    group_index = lax.axis_index("grp")
    half_index = group_index // (groups // 2)
    base = group_index * blk

    owners = groups // lax.axis_size("col")
    chunks = 2 if wide >= 256 else 1
    share = wide // owners // chunks
    own = [
        jnp.concatenate(
            [window_rows[:, (o * chunks + k) * share : (o * chunks + k + 1) * share] for o in range(owners)],
            axis=1,
        )
        for k in range(chunks)
    ]

    partner_source = partner_2(source, "grp", half_bit)
    partner = []
    for k in range(chunks):
        sent = own[k]
        if k > 0:
            sent, partner[k - 1] = lax.optimization_barrier((sent, partner[k - 1]))
        partner.append(partner_2(sent, "grp", half_bit))

    inverse = invert(base, source, partner_source)
    crossed = inverse >= blk
    kept = (base + jnp.arange(blk, dtype=jnp.int32)) < kept_count[0]
    masks = [kept & (crossed == (half_index != half)) for half in range(halves)]

    parts = []
    for k in range(chunks):
        arrived = partner[k]
        if k > 0:
            arrived, terms = lax.optimization_barrier((arrived, terms))
            parts.append(scatter_sum(terms))
        picked = pick_rows(inverse, own[k], arrived)
        rows = lax.all_gather(picked, "col", axis=1, tiled=True)
        terms = [
            lax.dot_general(
                jnp.where(mask[:, None], rows, jnp.zeros((), rows.dtype)),
                secular,
                (((0,), (0,)), ((), ())),
                preferred_element_type=jnp.float32,
            )
            for mask in masks
        ]
    parts.append(scatter_sum(terms))
    return jnp.concatenate(parts, axis=1).astype(jnp.bfloat16)


def solution(mesh):
    return jax.shard_map(
        per_device,
        mesh=mesh,
        in_specs=(P("grp", "col"), P("grp", "col"), P("grp"), P()),
        out_specs=P(None, "grp", "col"),
        check_vma=False,
    )
```

time: 1910 us -> 790 us (0.41)
  waiting for transfers between devices: 1500 us -> 522 us
  local copies, waits for them, and re-layouts: 282 us -> 12.4 us
  Pallas kernels: 0 us -> 126 us
  matrix products: 43.6 us -> 94.3 us
  other arithmetic: 63.6 us -> 16.2 us
    ppermute x1 -> x3, waiting for transfers between devices: 1350 us -> 190 us  [partner_2(): return lax.ppermute(value, axis, pairs)]
    gather x1 -> x0, local copies, waits for them, and re-layouts: 281 us -> none  [per_device(): stacked[picks]]
    all_gather x1 -> x2, waiting for transfers between devices: 0.01 us -> 199 us  [per_device(): rows = lax.all_gather(picked, 'col', axis=1, tiled=True)]
    pallas_call x0 -> x3, Pallas kernels: none -> 126 us  [the longest x1 86.1 us: invert(): pl.pallas_call(functools.partial(invert_kernel, blk), out_shape=jax.Shape...]
    dot_general x1 -> x4, matrix products: 43.6 us -> 94.3 us  [per_device(): lax.dot_general(jnp.where(mask[:, None], rows, jnp.zeros((), rows.dtype))...]
    concatenate x1 -> x3, other arithmetic: 56.5 us -> 7.73 us  [the longest x2 6.9 us: per_device(): jnp.concatenate([window_rows[:, (o * chunks + k) * share:(o * chunks + k...]
    reduce_scatter x1 -> x2, waiting for transfers between devices: 151 us -> 133 us  [scatter_sum(): lax.psum_scatter(jnp.stack(terms), 'grp', scatter_dimension=1, tiled=True)]
  transfers between devices with their start and end apart: 3 -> 7, of which waited for: 2 -> 6; matrix products, arithmetic and copies ran while one was open for 18% -> 13% of each run, Pallas kernels for 0% -> 11%
where the time goes in v1:
time: 790 us
  waiting for transfers between devices  522 us (66%)
  Pallas kernels  126 us (16%)
  matrix products  94.3 us (12%)
  other arithmetic  16.2 us (2%)
  between operations  13.9 us (2%)
  local copies, waits for them, and re-layouts  12.4 us (2%)
    all_gather x2, waiting for transfers between devices, per_device(): rows = lax.all_gather(picked, 'col', axis=1, tiled=True)  199 us
    ppermute x3, waiting for transfers between devices, partner_2(): return lax.ppermute(value, axis, pairs)  190 us
    reduce_scatter x2, waiting for transfers between devices, scatter_sum(): lax.psum_scatter(jnp.stack(terms), 'grp', scatter_dimension=1, tiled=True)  133 us
    dot_general x4, matrix products, per_device(): lax.dot_general(jnp.where(mask[:, None], rows, jnp.zeros((), rows.dtype))...  94.3 us
    pallas_call x1, Pallas kernels, invert(): pl.pallas_call(functools.partial(invert_kernel, blk), out_shape=jax.Shape...  86.1 us
    pallas_call x2, Pallas kernels, pick_rows(): pl.pallas_call(functools.partial(pick_kernel, blk), out_shape=jax.ShapeDt...  40 us
  transfers between devices with their start and end apart: 7, of which 6 were waited for; matrix products, arithmetic and copies ran while one was open for 13% of the time, Pallas kernels for 11%

profile of v1, /device:TPU:0, one launch (start us, length us, event | category | flops | bytes accessed | tf_op | source)
XLA Modules:
  0.0 789.9 jit_solution(3240870391652578981)
XLA Ops:
  6.5 7.1 fusion.28
  13.6 3.5 pad_maximum_fusion.3.own_ref
  17.1 4.0 collective-permute-start
  21.1 0.0 collective-permute-start.2
  21.2 3.4 pad_maximum_fusion.2.own_ref
  24.6 168.6 %collective-permute-done.2.partner_ref = s32[15360]{0:T(1024)S(1)} collective-permute-done((s32[15360]{0:T(1024)S(1)}, s32[15360]{0:T(1024)S(1)}, u32[]{:S(2)}, u32[]{:S(2)}) %collective-permute-start.2) | collective-permute-done | bytes 61472 | tf_op jit(solution)/shard_map/ppermute | solution.py:17
  193.2 0.6 copy-done.5
  193.8 86.1 %shard_map.46 = s32[15488]{0:T(1024)} custom-call(s32[1]{0:T(128)} %bitcast.1.base_ref, s32[15360]{0:T(1024)} %own_ref.1, s32[15360]{0:T(1024)} %copy-done.5), custom_call_target="tpu_custom_call" | custom-call | flops 122880 | bytes 184320 | tf_op jit(solution)/shard_map/pallas_call | solution.py:41
  279.9 0.8 slice.20.inverse_ref
  280.7 20.6 %shard_map.47 = bf16[15360,128]{1,0:T(8,128)(2,1)S(1)} custom-call(s32[15360]{0:T(1024)S(1)} %slice.20.inverse_ref, bf16[15360,128]{1,0:T(8,128)(2,1)} %pad_maximum_fusion.3.own_ref, bf16[15360,128]{1,0:T(8,128)(2,1)} %collective-permute-done.partner_ref), custom_call_target="tpu_custom_call" | custom-call | flops 3932160 | bytes 125829120 | tf_op jit(solution)/shard_map/pallas_call | solution.py:73
  301.4 1.9 copy-done.1
  303.3 0.0 all-gather.3.cloned.1.call-update
  303.3 0.0 all-gather.5.cloned.1.call-start
  304.1 0.1 collective-permute-start.1
  304.2 102.5 %all-gather.3.cloned.1.call-done = bf16[15360,512]{1,0:T(8,128)(2,1)} async-done(((bf16[15360,128]{1,0:T(8,128)(2,1)}), bf16[15360,512]{1,0:T(8,128)(2,1)}) %all-gather.3.cloned.1.call-update) | async-done | bytes 15728656 | tf_op jit(solution)/shard_map/all_gather | solution.py:131
  406.7 23.2 %fusion.4 = f32[512,1024]{1,0:T(8,128)S(1)} fusion(bf16[15360,1024]{1,0:T(8,128)(2,1)} %param.5, bf16[15360,512]{1,0:T(8,128)(2,1)} %all-gather.3.cloned.1.call-done, pred[15360]{0:T(1024)(128)(4,1)S(1)} %get-tuple-element.15), kind=kOutput, calls=%fused_computation.4 | convolution fusion | flops 16113991680 | bytes 49298432 | tf_op jit(solution)/shard_map/dot_general | solution.py:133
  429.9 24.3 %fusion.6 = f32[512,1024]{1,0:T(8,128)} fusion(bf16[15360,1024]{1,0:T(8,128)(2,1)} %param.5, bf16[15360,512]{1,0:T(8,128)(2,1)S(1)} %copy-done.6, pred[15360]{0:T(1024)(128)(4,1)S(1)} %fusion.23), kind=kOutput, calls=%fused_computation.6 | convolution fusion | flops 16113991680 | bytes 49298432 | tf_op jit(solution)/shard_map/dot_general | solution.py:133
  454.3 21.7 %collective-permute-done.1.partner_ref = bf16[15360,128]{1,0:T(8,128)(2,1)} collective-permute-done((bf16[15360,128]{1,0:T(8,128)(2,1)}, bf16[15360,128]{1,0:T(8,128)(2,1)}, u32[]{:S(2)}, u32[]{:S(2)}) %collective-permute-start.1) | collective-permute-done | bytes 3932192 | tf_op jit(solution)/shard_map/ppermute | solution.py:17
  475.9 19.4 %shard_map.48 = bf16[15360,128]{1,0:T(8,128)(2,1)S(1)} custom-call(s32[15360]{0:T(1024)S(1)} %slice.20.inverse_ref, bf16[15360,128]{1,0:T(8,128)(2,1)S(1)} %copy-done, bf16[15360,128]{1,0:T(8,128)(2,1)} %collective-permute-done.1.partner_ref), custom_call_target="tpu_custom_call" | custom-call | flops 3932160 | bytes 125829120 | tf_op jit(solution)/shard_map/pallas_call | solution.py:73
  495.3 1.9 copy-done.2
  497.3 0.0 reduce-scatter.3.cloned.1.call-start
  497.3 4.0 pad_maximum_fusion
  501.3 0.2 reduce-scatter.5.cloned.1.call-start
  501.6 96.5 %all-gather.5.cloned.1.call-done = bf16[15360,512]{1,0:T(8,128)(2,1)} async-done(((bf16[15360,128]{1,0:T(8,128)(2,1)}), bf16[15360,512]{1,0:T(8,128)(2,1)}) %all-gather.5.cloned.1.call-update) | async-done | bytes 15728656 | tf_op jit(solution)/shard_map/all_gather | solution.py:131
  598.1 23.4 %fusion.19 = f32[1,512,1024]{2,1,0:T(8,128)S(1)} fusion(bf16[15360,1024]{1,0:T(8,128)(2,1)} %param.5, bf16[15360,512]{1,0:T(8,128)(2,1)} %all-gather.5.cloned.1.call-done, pred[15360]{0:T(1024)(128)(4,1)S(1)} %get-tuple-element.15), kind=kOutput, calls=%fused_computation.21 | convolution fusion | flops 16113991680 | bytes 49298432 | tf_op jit(solution)/shard_map/dot_general | solution.py:133
  621.5 23.4 %fusion.16 = f32[1,512,1024]{2,1,0:T(8,128)S(1)} fusion(bf16[15360,1024]{1,0:T(8,128)(2,1)} %param.5, bf16[15360,512]{1,0:T(8,128)(2,1)S(1)} %copy-done.7, pred[15360]{0:T(1024)(128)(4,1)S(1)} %fusion.23), kind=kOutput, calls=%fused_computation.20 | convolution fusion | flops 16113991680 | bytes 49298432 | tf_op jit(solution)/shard_map/dot_general | solution.py:133
  644.9 2.3 pad_maximum_fusion.1
  647.3 42.5 %reduce-scatter.3.cloned.1.call-done = f32[2,64,1024]{2,1,0:T(8,128)} async-done(((f32[2,512,1024]{2,1,0:T(8,128)}), f32[2,64,1024]{2,1,0:T(8,128)}) %reduce-scatter.3.cloned.1.call-update) | async-done | bytes 524304 | tf_op jit(solution)/shard_map/reduce_scatter | solution.py:88
  689.8 1.1 convert.6
  690.9 90.5 %reduce-scatter.5.cloned.1.call-done = f32[2,64,1024]{2,1,0:T(8,128)} async-done(((f32[2,512,1024]{2,1,0:T(8,128)}), f32[2,64,1024]{2,1,0:T(8,128)}) %reduce-scatter.5.cloned.1.call-update) | async-done | bytes 524304 | tf_op jit(solution)/shard_map/reduce_scatter | solution.py:88
  781.4 1.1 convert.7
  782.5 0.8 pad_maximum_fusion.4
  (20 shorter events, 0.1 us)
Async XLA Ops:
  6.5 400.2 %all-gather.3.cloned.1.call-start = ((), (), s32[]{:S(2)}) async-start(), calls=%async_computation.2 | async-start | bytes 19660800 | tf_op jit(solution)/shard_map/all_gather | solution.py:131
  13.6 7.5 copy-start.4
  17.1 263.6 %collective-permute-start = (bf16[15360,128]{1,0:T(8,128)(2,1)}, bf16[15360,128]{1,0:T(8,128)(2,1)}, u32[]{:S(2)}, u32[]{:S(2)}) collective-permute-start(bf16[15360,128]{1,0:T(8,128)(2,1)} %pad_maximum_fusion.3.own_ref), channel_id=1, source_target_pairs={{0,16},{4,20},{8,24},{12,28},{16,0},{20,4},{24,8},{28,12},{1,17},{... | collective-permute-start | bytes 11796488 | tf_op jit(solution)/shard_map/ppermute | solution.py:17
  21.1 172.1 %collective-permute-start.2 = (s32[15360]{0:T(1024)S(1)}, s32[15360]{0:T(1024)S(1)}, u32[]{:S(2)}, u32[]{:S(2)}) collective-permute-start(s32[15360]{0:T(1024)S(1)} %copy-done.4), channel_id=1, source_target_pairs={{0,16},{4,20},{8,24},{12,28},{16,0},{20,4},{24,8},{28,12},{1,17},{... | collective-permute-start | bytes 184328 | tf_op jit(solution)/shard_map/ppermute | solution.py:17
  193.2 0.6 copy-start.5
  280.7 23.3 %copy-start.3 = (s32[15488]{0:T(1024)S(1)}, s32[15488]{0:T(1024)}, u32[]{:S(2)}) copy-start(s32[15488]{0:T(1024)} %shard_map.46) | copy-start | bytes 185860
  301.4 1.9 copy-start.1
  303.3 294.8 %all-gather.5.cloned.1.call-start = ((), (), s32[]{:S(2)}) async-start(), calls=%async_computation.4 | async-start | bytes 19660800 | tf_op jit(solution)/shard_map/all_gather | solution.py:131
  304.1 171.8 %collective-permute-start.1 = (bf16[15360,128]{1,0:T(8,128)(2,1)}, bf16[15360,128]{1,0:T(8,128)(2,1)}, u32[]{:S(2)}, u32[]{:S(2)}) collective-permute-start(bf16[15360,128]{1,0:T(8,128)(2,1)} %pad_maximum_fusion.2.own_ref), channel_id=1, source_target_pairs={{0,16},{4,20},{8,24},{12,28},{16,0},{20,4},{24,8},{28,12},{1,17},{... | collective-permute-start | bytes 11796488 | tf_op jit(solution)/shard_map/ppermute | solution.py:17
  406.7 23.2 %copy-start.6 = (bf16[15360,512]{1,0:T(8,128)(2,1)S(1)}, bf16[15360,512]{1,0:T(8,128)(2,1)}, u32[]{:S(2)}) copy-start(bf16[15360,512]{1,0:T(8,128)(2,1)} %all-gather.3.cloned.1.call-done) | copy-start | bytes 47185924
  429.9 46.0 %copy-start = (bf16[15360,128]{1,0:T(8,128)(2,1)S(1)}, bf16[15360,128]{1,0:T(8,128)(2,1)}, u32[]{:S(2)}) copy-start(bf16[15360,128]{1,0:T(8,128)(2,1)} %pad_maximum_fusion.2.own_ref) | copy-start | bytes 11796484
  495.3 1.9 copy-start.2
  497.3 192.6 %reduce-scatter.3.cloned.1.call-start = ((), (), s32[]{:S(2)}) async-start(), calls=%async_computation.3 | async-start | bytes 4718592 | tf_op jit(solution)/shard_map/reduce_scatter | solution.py:88
  501.3 280.1 %reduce-scatter.5.cloned.1.call-start = ((), (), s32[]{:S(2)}) async-start(), calls=%async_computation.5 | async-start | bytes 4718592 | tf_op jit(solution)/shard_map/reduce_scatter | solution.py:88
  598.1 23.4 %copy-start.7 = (bf16[15360,512]{1,0:T(8,128)(2,1)S(1)}, bf16[15360,512]{1,0:T(8,128)(2,1)}, u32[]{:S(2)}) copy-start(bf16[15360,512]{1,0:T(8,128)(2,1)} %all-gather.5.cloned.1.call-done) | copy-start | bytes 47185924
Sparse Core Ops, SparseCore 0:
  303.4 103.2 all-gather.2
  497.4 100.6 all-gather.4
  601.7 88.0 reduce-scatter.2
  693.8 87.6 reduce-scatter.4
